TPU v7x, 512 devices: a whole 4x4x16 slice. The times are simulated.
512 devices in a mesh: wide: 64 (over z_hi, x, y), narrow: 8 (over z_lo, core).
Axes of the slice: x: 4, y: 4, z: 16 (z_hi: 4, z_lo: 4; z = z_hi * 4 + z_lo), core: 2. Of those that a mesh axis runs over, the one named last changes fastest.
Arguments:
- initial_state: float32 [33554432], P(('wide', 'narrow')), may hold values from -6 to 6
- angles: float32 [3, 25], replicated, may hold values from -3.140625 to 3.140625
- pairings: int32 [3, 25], replicated, may hold values from 0 to 24, each once within a row
Outputs:
- final_state: float32 [33554432], P(('wide', 'narrow'))
Inputs may be any that keep to these rules, and one draw needn't show every extreme that they name: Each row of pairings names every qubit once.
All inputs are finite; a program needn't handle non-finite values.
Results may differ from a plain program's by a relative error of at most 0.00025.
Values sent between devices are 32-bit elements; how exact they have to be, the bound alone decides.
No kernel may reach another device: no remote copies, remote signals or barrier semaphores. Data moves between devices by JAX's collectives and lax.ppermute only.
A program may use at most 64 MiB of HBM per device.

v0:
```python
import functools

import jax
import jax.numpy as jnp
from jax import lax
from jax.experimental import pallas as pl
from jax.experimental.pallas import tpu as pltpu
from jax.sharding import PartitionSpec as P

SIDE = 256
LANES = 128
LOCAL = 16
PAIRS = 12
AXES = ("wide", "narrow")
LANE_PLACES = list(range(7))
ROW_PLACES = list(range(7, 15))
HALF = 15
DEVICE_ROWS = list(range(16, 24))
DEVICE_HALF = 24


def trig(angle):
    t = angle * 0.5
    u = t * t
    sine = 1.0 / 6227020800
    for term in (-1.0 / 39916800, 1.0 / 362880, -1.0 / 5040, 1.0 / 120, -1.0 / 6, 1.0):
        sine = sine * u + term
    cosine = -1.0 / 87178291200
    for term in (1.0 / 479001600, -1.0 / 3628800, 1.0 / 40320, -1.0 / 720, 1.0 / 24, -0.5, 1.0):
        cosine = cosine * u + term
    return cosine, sine * t


def iota(shape, axis):
    return lax.broadcasted_iota(jnp.int32, shape, axis)


def choose_trades(bound):
    free = ~bound & 127
    stuck = jnp.int32(0)
    trades = []
    for place in range(7, 16):
        wanted = bound & (1 << place)
        taken = jnp.where(wanted != 0, free & -free, 0)
        stuck = stuck | jnp.where(taken == 0, wanted, 0)
        free = free & ~taken
        trades.append(taken)
    return trades, stuck


def partners_of(pairings, layer, mask):
    found = jnp.int32(0)
    one = jnp.int32(1)
    for k in range(PAIRS):
        p, r = pairings[layer, 2 * k], pairings[layer, 2 * k + 1]
        found = found | lax.shift_left(lax.shift_right_logical(mask, r) & one, p)
        found = found | lax.shift_left(lax.shift_right_logical(mask, p) & one, r)
    return found


def qubits_at(trades):
    table = []
    for lane in range(7):
        held = jnp.int32(lane)
        for place in range(7, 16):
            held = jnp.where(trades[place - 7] == 1 << lane, place, held)
        table.append(held)
    for place in range(7, 16):
        taken = trades[place - 7]
        held = jnp.int32(0)
        for lane in range(1, 7):
            held = held + jnp.where(taken >= 1 << lane, 1, 0)
        table.append(jnp.where(taken == 0, place, held))
    return table


def angle_table(entries):
    spot = iota((8, LANES), 0) * LANES + iota((8, LANES), 1)
    table = jnp.zeros((8, LANES), jnp.float32)
    for row, lane, value in entries:
        table = jnp.where(spot == row * LANES + lane, value, table)
    return table


def bit_masks():
    i, j = iota((LANES, LANES), 0), iota((LANES, LANES), 1)
    same = [((i ^ j) >> b) & 1 == 0 for b in range(7)]
    upper = [(i >> b) & 1 == 1 for b in range(7)]
    return same, upper


def kron_matrix(masks, turns, row, places, transposed):
    same, upper = masks
    cosines, sines = turns

    def turn(place):
        c = cosines[row : row + 1, place : place + 1]
        s = sines[row : row + 1, place : place + 1]
        return c, -s if transposed else s

    total = None
    for b in range(7):
        c, s = turn(places[b])
        factor = jnp.where(same[b], c, jnp.where(upper[b], s, -s))
        total = factor if total is None else total * factor
    c, s = turn(places[7])
    top = jnp.concatenate([total * c, total * -s], axis=1)
    low = jnp.concatenate([total * s, total * c], axis=1)
    return parts(jnp.concatenate([top, low], axis=0))


def parts(value):
    high = value.astype(jnp.bfloat16)
    low = (value - high.astype(jnp.float32)).astype(jnp.bfloat16)
    return high, low


def product(left, right):
    (lh, ll), (rh, rl) = left, right

    def dot(a, b):
        return jnp.dot(a, b, preferred_element_type=jnp.float32)

    return dot(lh, rh) + (dot(lh, rl) + dot(ll, rh))


def on_rows(matrix, value):
    return product(matrix, parts(value))


def on_columns(value, matrix):
    return product(parts(value), matrix)


def turn_halves(turns, row, place, value):
    cosines, sines = turns
    c = cosines[row : row + 1, place : place + 1]
    s = sines[row : row + 1, place : place + 1]
    first, second = value[:, :LANES], value[:, LANES:]
    return jnp.concatenate([c * first - s * second, s * first + c * second], axis=1)


def load_matrix(ref):
    return jnp.concatenate([ref[:SIDE, :], ref[SIDE:, :]], axis=1)


def store_matrix(ref, value):
    ref[:SIDE, :] = value[:, :LANES]
    ref[SIDE:, :] = value[:, LANES:]


def sign_array(pairs, keep, device=None):
    def shifts(shape, axis):
        spot = iota(shape, axis)
        p = jnp.full(shape, -1, jnp.int32)
        r = p
        for k, (first, second) in enumerate(pairs):
            p = jnp.where(spot == k, first, p)
            r = jnp.where(spot == k, second, r)
        applies = jnp.where((p >= 0) & keep(p, r), 1, 0)
        if device is not None:
            held = jnp.full(shape, device, jnp.int32)
            for place in (p, r):
                bit = lax.shift_right_logical(held, jnp.maximum(place - LOCAL, 0)) & 1
                applies = applies & jnp.where(place >= LOCAL, bit, 1)
        return p, r, applies

    def row_bit(place, applies):
        inside = (place >= 7) & (place < HALF)
        return jnp.where(applies == 1, jnp.where(inside, place - 7, 8), 31)

    def column_bit(place):
        return jnp.where(place < 7, place, jnp.where(place == HALF, 7, 8))

    p, r, applies = shifts((1, 16), 1)
    row = iota((SIDE, 16), 0) | SIDE
    row = lax.shift_right_logical(row, jnp.broadcast_to(row_bit(p, applies), row.shape)) & (
        lax.shift_right_logical(row, jnp.broadcast_to(row_bit(r, applies), row.shape))
    )
    p, r, _ = shifts((16, 1), 0)
    column = iota((16, SIDE), 1) | SIDE
    column = lax.shift_right_logical(column, jnp.broadcast_to(column_bit(p), column.shape)) & (
        lax.shift_right_logical(column, jnp.broadcast_to(column_bit(r), column.shape))
    )
    count = jnp.dot(
        (row & 1).astype(jnp.float32).astype(jnp.bfloat16),
        (column & 1).astype(jnp.float32).astype(jnp.bfloat16),
        preferred_element_type=jnp.float32,
    )
    return (1 - 2 * (count.astype(jnp.int32) & 1)).astype(jnp.float32)


def has_device(p, r):
    return (p >= LOCAL) | (r >= LOCAL)


def all_local(p, r):
    return (p < LOCAL) & (r < LOCAL)


def trade_bits(work, trades):
    lane = iota((SIDE, LANES), 1)
    row = iota((SIDE, LANES), 0)
    for bit in range(8):
        taken = trades[bit]
        step = 1 << bit

        @pl.when(taken != 0)
        def _():
            lane_up = (lane & taken) != 0
            row_up = (row & step) != 0
            for half in range(2):
                columns = slice(half * LANES, half * LANES + LANES)
                held = work[:, columns]
                from_later = pltpu.roll(pltpu.roll(held, SIDE - step, 0), taken, 1)
                from_sooner = pltpu.roll(pltpu.roll(held, step, 0), LANES - taken, 1)
                moved = jnp.where(lane_up, from_later, from_sooner)
                work[:, columns] = jnp.where(row_up == lane_up, held, moved)

    taken = trades[8]

    @pl.when(taken != 0)
    def _():
        lane_up = (lane & taken) != 0
        first = work[:, :LANES]
        second = work[:, LANES:]
        work[:, :LANES] = jnp.where(lane_up, pltpu.roll(second, taken, 1), first)
        work[:, LANES:] = jnp.where(lane_up, second, pltpu.roll(first, LANES - taken, 1))


def first_kernel(angles_in, pairings_in, state_in, out, plan, work, state, angles, pairings, arrived):
    copies = [
        pltpu.make_async_copy(source, target, arrived.at[slot])
        for slot, (source, target) in enumerate(
            ((angles_in, angles), (pairings_in, pairings), (state_in, state))
        )
    ]
    for copy in copies:
        copy.start()
    for copy in copies:
        copy.wait()
    of_device = jnp.int32(((1 << 25) - 1) - ((1 << LOCAL) - 1))
    apart = partners_of(pairings, 0, of_device)
    bound = apart & partners_of(pairings, 1, of_device) & ((1 << LOCAL) - 1)
    trades, stuck = choose_trades(bound)
    held = qubits_at(trades)
    plan[0] = stuck
    plan[1] = apart
    for place in range(LOCAL):
        plan[2 + place] = held[place]
    for bit in range(9):
        plan[18 + bit] = trades[bit]
    entries = [(0, q, angles[0, q]) for q in range(LOCAL)]
    for place in range(7, LOCAL):
        late = lax.shift_right_logical(apart, held[place]) & 1
        entries.append((1, place, jnp.where(late == 1, 0.0, angles[1, held[place]])))
    turns = trig(angle_table(entries))
    masks = bit_masks()
    rows = kron_matrix(masks, turns, 0, ROW_PLACES, False)
    columns = kron_matrix(masks, turns, 0, LANE_PLACES + [HALF], True)
    early = kron_matrix(masks, turns, 1, ROW_PLACES, False)
    pairs = [(pairings[0, 2 * k], pairings[0, 2 * k + 1]) for k in range(PAIRS)]
    sign = sign_array(pairs, all_local)
    value = on_columns(on_rows(rows, load_matrix(state)), columns) * sign
    work[...] = value
    trade_bits(work, trades)
    value = on_rows(early, work[...])
    store_matrix(out, turn_halves(turns, 1, HALF, value))


DEVICE_1, DEVICE_2, DEVICE_3, COLUMN_2, ROW_2, ROW_3, COLUMN_3 = range(7)
SIGN_1, SIGN_2, SIGN_LATE, SIGN_3 = range(4)


def prepare_kernel(angles, pairings, plan, high, low, sign, table, places):
    stuck, apart = plan[0], plan[1]
    held = [plan[2 + place] for place in range(LOCAL)]
    waiting = partners_of(pairings, 1, stuck)
    for place in range(LOCAL):
        places[held[place]] = jnp.int32(place)
    for place in range(LOCAL, 25):
        places[place] = jnp.int32(place)
    entries = []
    for p in range(LOCAL, 25):
        waits = (waiting >> p) & 1 == 1
        entries += [(0, p, angles[0, p]), (1, p, angles[1, p])]
        entries.append((2, p, jnp.where(waits, 0.0, angles[2, p])))
        entries.append((3, p, jnp.where(waits, angles[2, p], 0.0)))
    for p in range(7):
        entries += [(1, p, angles[1, held[p]]), (2, p, angles[2, held[p]])]
    for p in range(7, LOCAL):
        late = lax.shift_right_logical(apart, held[p]) & 1
        entries.append((1, p, jnp.where(late == 1, angles[1, held[p]], 0.0)))
        entries.append((2, p, angles[2, held[p]]))
    turns = trig(angle_table(entries))
    table[0:8, :], table[8:16, :] = turns
    masks = bit_masks()
    for slot, layer, spots, transposed in (
        (DEVICE_1, 0, DEVICE_ROWS, False),
        (DEVICE_2, 1, DEVICE_ROWS, False),
        (DEVICE_3, 2, DEVICE_ROWS, False),
        (COLUMN_2, 1, LANE_PLACES + [DEVICE_HALF], True),
        (ROW_2, 1, ROW_PLACES, False),
        (ROW_3, 2, ROW_PLACES, False),
        (COLUMN_3, 2, LANE_PLACES + [HALF], True),
    ):
        high[slot], low[slot] = kron_matrix(masks, turns, layer, spots, transposed)
    device = lax.axis_index("wide") * lax.axis_size("narrow") + lax.axis_index("narrow")

    def pairs_of(layer, inner):
        pairs = []
        for k in range(2 * PAIRS):
            place = places[pairings[layer, k]]
            if inner:
                moved = jnp.where(place >= LOCAL, place - 9, place + 9)
                place = jnp.where(place < 7, place, moved)
            pairs.append(place)
        return list(zip(pairs[::2], pairs[1::2]))

    def is_stuck(place):
        mask = jnp.full(place.shape, stuck, jnp.int32)
        return (lax.shift_right_logical(mask, jnp.maximum(place, 0)) & 1) == 1

    def local_or_stuck(p, r):
        return all_local(p, r) | is_stuck(p) | is_stuck(r)

    def on_device(p, r):
        return ((p >= 7) & (p < LOCAL)) | ((r >= 7) & (r < LOCAL))

    def on_device_not_stuck(p, r):
        return on_device(p, r) & ~(is_stuck(p - 9) | is_stuck(r - 9))

    sign[SIGN_1] = sign_array(pairs_of(0, True), on_device, device)
    sign[SIGN_2] = sign_array(pairs_of(1, True), on_device_not_stuck, device)
    sign[SIGN_LATE] = sign_array(pairs_of(1, False), local_or_stuck, device)
    sign[SIGN_3] = sign_array(pairs_of(2, False), lambda p, r: p == p, device)


def second_kernel(state, high, low, sign, table, out):
    def matrix(slot):
        return high[slot], low[slot]

    turns = table[0:8, :], table[8:16, :]
    value = on_rows(matrix(DEVICE_1), load_matrix(state))
    value = turn_halves(turns, 0, DEVICE_HALF, value) * sign[SIGN_1]
    value = on_columns(on_rows(matrix(DEVICE_2), value), matrix(COLUMN_2)) * sign[SIGN_2]
    value = on_rows(matrix(DEVICE_3), value)
    store_matrix(out, turn_halves(turns, 2, DEVICE_HALF, value))


def third_kernel(front, back, plan, high, low, sign, table, state, out, work):
    def matrix(slot):
        return high[slot], low[slot]

    turns = table[0:8, :], table[8:16, :]
    value = load_matrix(state)
    if front:
        value = on_rows(matrix(ROW_2), value)
        value = turn_halves(turns, 1, HALF, value) * sign[SIGN_LATE]
        value = on_columns(on_rows(matrix(ROW_3), value), matrix(COLUMN_3))
    if back:
        work[...] = value * sign[SIGN_3]
        trade_bits(work, [plan[18 + bit] for bit in range(9)])
        value = work[...]
    store_matrix(out, value)


def call(kernel, in_spaces, out_shapes, scratch, flops, limit):
    specs = [pl.BlockSpec(memory_space=space) for space in in_spaces]
    outs = [jax.ShapeDtypeStruct(shape, dtype) for shape, dtype, _ in out_shapes]
    out_specs = [pl.BlockSpec(memory_space=space) for _, _, space in out_shapes]
    return pl.pallas_call(
        kernel,
        in_specs=specs,
        out_shape=outs,
        out_specs=out_specs,
        scratch_shapes=scratch,
        compiler_params=pltpu.CompilerParams(vmem_limit_bytes=limit * 1024 * 1024),
        cost_estimate=pl.CostEstimate(flops=flops, bytes_accessed=4_000_000, transcendentals=0),
    )


def shards(initial_state, angles, pairings):
    V, S = pltpu.VMEM, pltpu.SMEM
    rows = 2 * SIDE
    flat = ((rows, LANES), jnp.float32, V)
    work = [pltpu.VMEM((SIDE, SIDE), jnp.float32)]
    product_flops = 3 * 2 * SIDE**3

    def across(value):
        return lax.all_to_all(value, AXES, 0, 0, tiled=True)

    fetched = [
        pltpu.VMEM((rows, LANES), jnp.float32),
        pltpu.SMEM(angles.shape, jnp.float32),
        pltpu.SMEM(pairings.shape, jnp.int32),
        pltpu.SemaphoreType.DMA((3,)),
    ]
    state, plan = call(
        first_kernel,
        [pltpu.HBM] * 3,
        [flat, ((27,), jnp.int32, S)],
        work + fetched,
        3 * product_flops,
        60,
    )(angles, pairings, initial_state.reshape(rows, LANES))
    state = across(state)
    prepared = call(
        prepare_kernel,
        [S, S, S],
        [
            ((7, SIDE, SIDE), jnp.bfloat16, V),
            ((7, SIDE, SIDE), jnp.bfloat16, V),
            ((4, SIDE, SIDE), jnp.float32, V),
            ((16, LANES), jnp.float32, V),
        ],
        [pltpu.SMEM((25,), jnp.int32)],
        40 * product_flops,
        32,
    )(angles, pairings, plan)
    stuck = plan[0] != 0
    state, stuck, prepared = lax.optimization_barrier((state, stuck, prepared))
    (state,) = call(second_kernel, [V] * 5, [flat], [], 4 * product_flops, 32)(state, *prepared)
    state = across(state)

    def third(value, front, back):
        kernel = functools.partial(third_kernel, front, back)
        return call(kernel, [S] + [V] * 5, [flat], work, 3 * product_flops, 32)(
            plan, *prepared, value
        )[0]

    def finish(value):
        return third(value, True, True).reshape(-1)

    def finish_slowly(value):
        value = third(value, True, False)
        table = prepared[3]
        device = lax.axis_index(AXES)
        devices = lax.axis_size(AXES)
        for bit in range(9):
            route = [(d, d ^ 1 << bit) for d in range(devices)]
            other = lax.ppermute(value, AXES, route)
            c, s = table[3, LOCAL + bit], table[11, LOCAL + bit]
            upper = lax.shift_right_logical(device, bit) & 1 == 1
            value = c * value + jnp.where(upper, s, -s) * other
        return third(value, False, True).reshape(-1)

    return lax.cond(stuck, finish_slowly, finish, state)


def solution(mesh):
    return jax.shard_map(
        shards,
        mesh=mesh,
        in_specs=(P(AXES), P(), P()),
        out_specs=P(AXES),
        check_vma=False,
    )
```

profile of v0, /device:TPU:1, one launch (start us, length us, event | category | flops | bytes accessed | tf_op | source)
XLA Modules:
  0.0 89.4 jit_solution(9050079109596830510)
XLA Ops:
  0.0 3.3 %shard_map.39 = (f32[512,128]{1,0:T(8,128)}, s32[27]{0:T(128)S(1)}) custom-call(f32[3,25]{1,0:T(4,128)} %angles.1, s32[3,25]{1,0:T(4,128)} %pairings.1, f32[512,128]{1,0:T(8,128)} %bitcast.36), custom_call_target="tpu_custom_call" | custom-call | flops 301989888 | bytes 4000000 | tf_op jit(solution)/shard_map/pallas_call | solution.py:399
  3.3 0.0 copy-start.1
  3.3 24.3 %all-to-all-start = ((f32[512,1,128]{2,1,0:T(1,128)}), f32[512,1,128]{2,1,0:T(1,128)S(1)}, u32[]{:S(2)}, u32[]{:S(2)}) async-start(f32[512,1,128]{2,1,0:T(1,128)} %bitcast.34), calls=%async_computation | async-start | bytes 524288 | tf_op jit(solution)/shard_map/all_to_all | solution.py:391
  27.7 0.0 copy-start
  27.7 0.0 copy-done.1
  27.7 0.6 copy-done
  28.3 2.1 %shard_map.40 = (bf16[7,256,256]{2,1,0:T(8,128)(2,1)S(1)}, bf16[7,256,256]{2,1,0:T(8,128)(2,1)S(1)}, f32[4,256,256]{2,1,0:T(8,128)S(1)}, f32[16,128]{1,0:T(8,128)S(1)}) custom-call(f32[3,25]{1,0:T(4,128)S(1)} %copy-done, s32[3,25]{1,0:T(4,128)S(1)} %copy-done.1, s32[27]{0:T(128)S(1)} %get-tuple-element.57.plan), custom_call_target="tpu_custom_call" | custom-call | flops 4026531840 | bytes 4000000 | tf_op jit(solution)/shard_map/pallas_call | solution.py:408
  30.5 21.0 %all-to-all-done = f32[512,1,128]{2,1,0:T(1,128)S(1)} async-done(((f32[512,1,128]{2,1,0:T(1,128)}), f32[512,1,128]{2,1,0:T(1,128)S(1)}, u32[]{:S(2)}, u32[]{:S(2)}) %all-to-all-start) | async-done | bytes 262176 | tf_op jit(solution)/shard_map/all_to_all | solution.py:391
  51.4 2.0 %shard_map.41 = f32[512,128]{1,0:T(8,128)} custom-call(f32[512,128]{1,0:T(8,128)S(1)} %bitcast.31, bf16[7,256,256]{2,1,0:T(8,128)(2,1)S(1)} %get-tuple-element.63.high, bf16[7,256,256]{2,1,0:T(8,128)(2,1)S(1)} %get-tuple-element.64.low, f32[4,256,256]{2,1,0:T(8,128)S(1)} %get-tuple-element.65.sign, f32[16,128]{1,0:T(8,128)S(1)} %get-tuple-element.66.table), custom_call_target="tpu_custom_call" | custom-call | flops 402653184 | bytes 4000000 | tf_op jit(solution)/shard_map/pallas_call | solution.py:423
  53.4 9.6 %all-to-all-start.1 = ((f32[512,1,128]{2,1,0:T(1,128)}), f32[512,1,128]{2,1,0:T(1,128)S(1)}, u32[]{:S(2)}, u32[]{:S(2)}) async-start(f32[512,1,128]{2,1,0:T(1,128)} %bitcast.26), calls=%async_computation.1 | async-start | bytes 524288 | tf_op jit(solution)/shard_map/all_to_all | solution.py:391
  63.0 23.9 %all-to-all-done.1 = f32[512,1,128]{2,1,0:T(1,128)S(1)} async-done(((f32[512,1,128]{2,1,0:T(1,128)}), f32[512,1,128]{2,1,0:T(1,128)S(1)}, u32[]{:S(2)}, u32[]{:S(2)}) %all-to-all-start.1) | async-done | bytes 262176 | tf_op jit(solution)/shard_map/all_to_all | solution.py:391
  86.9 2.5 %conditional.1 = (f32[65536]{0:T(1024)}) conditional(s32[]{:T(128)} %convert_element_type.3, (s32[27]{0:T(128)S(1)}, bf16[7,256,256]{2,1,0:T(8,128)(2,1)S(1)}, bf16[7,256,256]{2,1,0:T(8,128)(2,1)S(1)}, f32[4,256,256]{2,1,0:T(8,128)S(1)}, f32[16,128]{1,0:T(8,128)S(1)}, /*index=5*/f32[512,128]{1,0:T(8,128)S(1)}) %tuple.36, (f32[16,128]{1,0:T(8,128)S(1)}, ...), branch_computations={%region_0.0_spmd, %region_1.2_spmd} | conditional | flops 605749248 | bytes 28710628 | solution.py:448
  86.9 2.5 %branch_0_fun.1 = f32[512,128]{1,0:T(8,128)} custom-call(s32[27]{0:T(128)S(1)} %get-tuple-element.32.plan, bf16[7,256,256]{2,1,0:T(8,128)(2,1)S(1)} %get-tuple-element.33.high, bf16[7,256,256]{2,1,0:T(8,128)(2,1)S(1)} %get-tuple-element.34.low, f32[4,256,256]{2,1,0:T(8,128)S(1)} %get-tuple-element.35.sign, f32[16,128]{1,0:T(8,128)S(1)} %get-tuple-element.36.table, ...), custom_call_target="tpu_custom_call" | custom-call | flops 301989888 | bytes 4000000 | tf_op jit(solution)/shard_map/cond/branch_0_fun/pallas_call | solution.py:428
Async XLA Ops:
  3.3 24.4 %copy-start.1 = (s32[3,25]{1,0:T(4,128)S(1)}, s32[3,25]{1,0:T(4,128)}, u32[]{:S(2)}) copy-start(s32[3,25]{1,0:T(4,128)} %pairings.1) | copy-start | bytes 904
  3.3 48.1 %all-to-all-start = ((f32[512,1,128]{2,1,0:T(1,128)}), f32[512,1,128]{2,1,0:T(1,128)S(1)}, u32[]{:S(2)}, u32[]{:S(2)}) async-start(f32[512,1,128]{2,1,0:T(1,128)} %bitcast.34), calls=%async_computation | async-start | bytes 524288 | tf_op jit(solution)/shard_map/all_to_all | solution.py:391
  27.7 0.7 copy-start
  53.4 33.5 %all-to-all-start.1 = ((f32[512,1,128]{2,1,0:T(1,128)}), f32[512,1,128]{2,1,0:T(1,128)S(1)}, u32[]{:S(2)}, u32[]{:S(2)}) async-start(f32[512,1,128]{2,1,0:T(1,128)} %bitcast.26), calls=%async_computation.1 | async-start | bytes 524288 | tf_op jit(solution)/shard_map/all_to_all | solution.py:391
where the time goes:
time: 89.6 us; the launch traced here: 89.4 us
  waiting for transfers between devices  44.9 us (50%)
  starting transfers between devices  33.9 us (38%)
  Pallas kernels  9.89 us (11%)
    all_to_all x2, waiting for transfers between devices, across(): return lax.all_to_all(value, AXES, 0, 0, tiled=True)  44.9 us
    all_to_all x2, starting transfers between devices, across(): return lax.all_to_all(value, AXES, 0, 0, tiled=True)  33.9 us
    pallas_call x1, Pallas kernels, shards(): call(first_kernel, [pltpu.HBM] * 3, [flat, ((27,), jnp.int32, S)], work +...  3.32 us
    pallas_call x1, Pallas kernels, third(): call(kernel, [S] + [V] * 5, [flat], work, 3 * product_flops, 32)  2.48 us
    pallas_call x1, Pallas kernels, shards(): call(prepare_kernel, [S, S, S], [((7, SIDE, SIDE), jnp.bfloat16, V), ((7,...  2.12 us
    pallas_call x1, Pallas kernels, shards(): call(second_kernel, [V] * 5, [flat], [], 4 * product_flops, 32)  1.98 us
  transfers between devices with their start and end apart: 2, of which 2 were waited for; matrix products, arithmetic and copies ran while one was open for 0% of the time, Pallas kernels for 2%

commit v1 on v0

--- a/solution.py
+++ b/solution.py
@@ -10,13 +10,15 @@
 SIDE = 256
 LANES = 128
 LOCAL = 16
+CORE = 16
+SIGNED_CORE = 25
 PAIRS = 12
+FLIP = 0b10101000
 AXES = ("wide", "narrow")
 LANE_PLACES = list(range(7))
 ROW_PLACES = list(range(7, 15))
 HALF = 15
-DEVICE_ROWS = list(range(16, 24))
-DEVICE_HALF = 24
+CHIP_PLACES = list(range(17, 25))
 
 
 def trig(angle):
@@ -36,10 +38,10 @@
 
 
 def choose_trades(bound):
-    free = ~bound & 127
+    free = (~bound & 127) | (lax.shift_right_logical(~bound, HALF) & 1) * LANES
     stuck = jnp.int32(0)
     trades = []
-    for place in range(7, 16):
+    for place in ROW_PLACES:
         wanted = bound & (1 << place)
         taken = jnp.where(wanted != 0, free & -free, 0)
         stuck = stuck | jnp.where(taken == 0, wanted, 0)
@@ -59,18 +61,12 @@
 
 
 def qubits_at(trades):
-    table = []
-    for lane in range(7):
-        held = jnp.int32(lane)
-        for place in range(7, 16):
-            held = jnp.where(trades[place - 7] == 1 << lane, place, held)
-        table.append(held)
-    for place in range(7, 16):
-        taken = trades[place - 7]
-        held = jnp.int32(0)
-        for lane in range(1, 7):
-            held = held + jnp.where(taken >= 1 << lane, 1, 0)
-        table.append(jnp.where(taken == 0, place, held))
+    table = [jnp.int32(place) for place in range(LOCAL)]
+    for lane in range(8):
+        own = HALF if lane == 7 else lane
+        for place in ROW_PLACES:
+            table[own] = jnp.where(trades[place - 7] == 1 << lane, place, table[own])
+            table[place] = jnp.where(trades[place - 7] == 1 << lane, own, table[place])
     return table
 
 
@@ -117,11 +113,9 @@
 
 def product(left, right):
     (lh, ll), (rh, rl) = left, right
-
-    def dot(a, b):
-        return jnp.dot(a, b, preferred_element_type=jnp.float32)
-
-    return dot(lh, rh) + (dot(lh, rl) + dot(ll, rh))
+    a = jnp.concatenate([lh, lh, ll], axis=1)
+    b = jnp.concatenate([rh, rl, rh], axis=0)
+    return jnp.dot(a, b, preferred_element_type=jnp.float32)
 
 
 def on_rows(matrix, value):
@@ -130,14 +124,6 @@
 
 def on_columns(value, matrix):
     return product(parts(value), matrix)
-
-
-def turn_halves(turns, row, place, value):
-    cosines, sines = turns
-    c = cosines[row : row + 1, place : place + 1]
-    s = sines[row : row + 1, place : place + 1]
-    first, second = value[:, :LANES], value[:, LANES:]
-    return jnp.concatenate([c * first - s * second, s * first + c * second], axis=1)
 
 
 def load_matrix(ref):
@@ -149,7 +135,17 @@
     ref[SIDE:, :] = value[:, LANES:]
 
 
-def sign_array(pairs, keep, device=None):
+def load_pieces(ref):
+    first, second = pl.ds(0, SIDE, stride=2), pl.ds(1, SIDE, stride=2)
+    return jnp.concatenate([ref[first, :], ref[second, :]], axis=1)
+
+
+def store_pieces(ref, value):
+    ref[pl.ds(0, SIDE, stride=2), :] = value[:, :LANES]
+    ref[pl.ds(1, SIDE, stride=2), :] = value[:, LANES:]
+
+
+def sign_array(pairs, keep, device=None, swapped=False):
     def shifts(shape, axis):
         spot = iota(shape, axis)
         p = jnp.full(shape, -1, jnp.int32)
@@ -158,6 +154,10 @@
             p = jnp.where(spot == k, first, p)
             r = jnp.where(spot == k, second, r)
         applies = jnp.where((p >= 0) & keep(p, r), 1, 0)
+        if swapped:
+            p, r = (
+                jnp.where(in_rows(x), x + 10, jnp.where(x > CORE, x - 10, x)) for x in (p, r)
+            )
         if device is not None:
             held = jnp.full(shape, device, jnp.int32)
             for place in (p, r):
@@ -166,14 +166,13 @@
         return p, r, applies
 
     def row_bit(place, applies):
-        inside = (place >= 7) & (place < HALF)
-        return jnp.where(applies == 1, jnp.where(inside, place - 7, 8), 31)
+        return jnp.where(applies == 1, jnp.where(in_rows(place), place - 7, 8), 31)
 
     def column_bit(place):
-        return jnp.where(place < 7, place, jnp.where(place == HALF, 7, 8))
+        return jnp.where((place >= 0) & (place < 7), place, jnp.where(place == HALF, 7, 8))
 
     p, r, applies = shifts((1, 16), 1)
-    row = iota((SIDE, 16), 0) | SIDE
+    row = iota((SIDE, 16), 0) ^ (FLIP if swapped else 0) | SIDE
     row = lax.shift_right_logical(row, jnp.broadcast_to(row_bit(p, applies), row.shape)) & (
         lax.shift_right_logical(row, jnp.broadcast_to(row_bit(r, applies), row.shape))
     )
@@ -190,8 +189,8 @@
     return (1 - 2 * (count.astype(jnp.int32) & 1)).astype(jnp.float32)
 
 
-def has_device(p, r):
-    return (p >= LOCAL) | (r >= LOCAL)
+def in_rows(place):
+    return (place >= 7) & (place < HALF)
 
 
 def all_local(p, r):
@@ -205,7 +204,15 @@
         taken = trades[bit]
         step = 1 << bit
 
-        @pl.when(taken != 0)
+        @pl.when(taken == LANES)
+        def _():
+            row_up = (row & step) != 0
+            first = work[:, :LANES]
+            second = work[:, LANES:]
+            work[:, :LANES] = jnp.where(row_up, pltpu.roll(second, step, 0), first)
+            work[:, LANES:] = jnp.where(row_up, second, pltpu.roll(first, SIDE - step, 0))
+
+        @pl.when((taken != 0) & (taken < LANES))
         def _():
             lane_up = (lane & taken) != 0
             row_up = (row & step) != 0
@@ -216,17 +223,6 @@
                 from_sooner = pltpu.roll(pltpu.roll(held, step, 0), LANES - taken, 1)
                 moved = jnp.where(lane_up, from_later, from_sooner)
                 work[:, columns] = jnp.where(row_up == lane_up, held, moved)
-
-    taken = trades[8]
-
-    @pl.when(taken != 0)
-    def _():
-        lane_up = (lane & taken) != 0
-        first = work[:, :LANES]
-        second = work[:, LANES:]
-        work[:, :LANES] = jnp.where(lane_up, pltpu.roll(second, taken, 1), first)
-        work[:, LANES:] = jnp.where(lane_up, second, pltpu.roll(first, LANES - taken, 1))
-
 
 def first_kernel(angles_in, pairings_in, state_in, out, plan, work, state, angles, pairings, arrived):
     copies = [
@@ -248,10 +244,10 @@
     plan[1] = apart
     for place in range(LOCAL):
         plan[2 + place] = held[place]
-    for bit in range(9):
+    for bit in range(8):
         plan[18 + bit] = trades[bit]
     entries = [(0, q, angles[0, q]) for q in range(LOCAL)]
-    for place in range(7, LOCAL):
+    for place in ROW_PLACES:
         late = lax.shift_right_logical(apart, held[place]) & 1
         entries.append((1, place, jnp.where(late == 1, 0.0, angles[1, held[place]])))
     turns = trig(angle_table(entries))
@@ -264,12 +260,11 @@
     value = on_columns(on_rows(rows, load_matrix(state)), columns) * sign
     work[...] = value
     trade_bits(work, trades)
-    value = on_rows(early, work[...])
-    store_matrix(out, turn_halves(turns, 1, HALF, value))
-
-
-DEVICE_1, DEVICE_2, DEVICE_3, COLUMN_2, ROW_2, ROW_3, COLUMN_3 = range(7)
-SIGN_1, SIGN_2, SIGN_LATE, SIGN_3 = range(4)
+    store_pieces(out, on_rows(early, work[...]))
+
+
+CHIP_1, CHIP_2, CHIP_3, COLUMN_2, ROW_2, ROW_3, COLUMN_3 = range(7)
+MINE_1, OTHER_1, MINE_2, OTHER_2, SIGN_LATE, SIGN_3 = range(6)
 
 
 def prepare_kernel(angles, pairings, plan, high, low, sign, table, places):
@@ -280,15 +275,23 @@
         places[held[place]] = jnp.int32(place)
     for place in range(LOCAL, 25):
         places[place] = jnp.int32(place)
+    device = lax.axis_index("wide") * lax.axis_size("narrow") + lax.axis_index("narrow")
+    core = device & 1
     entries = []
     for p in range(LOCAL, 25):
         waits = (waiting >> p) & 1 == 1
-        entries += [(0, p, angles[0, p]), (1, p, angles[1, p])]
-        entries.append((2, p, jnp.where(waits, 0.0, angles[2, p])))
         entries.append((3, p, jnp.where(waits, angles[2, p], 0.0)))
-    for p in range(7):
+        for layer in range(3):
+            angle = angles[layer, p]
+            if layer == 2:
+                angle = jnp.where(waits, 0.0, angle)
+            if p == CORE:
+                entries.append((layer, SIGNED_CORE, jnp.where(core == 1, angle, -angle)))
+            else:
+                entries.append((layer, p, -angle if FLIP >> (p - 17) & 1 else angle))
+    for p in LANE_PLACES + [HALF]:
         entries += [(1, p, angles[1, held[p]]), (2, p, angles[2, held[p]])]
-    for p in range(7, LOCAL):
+    for p in ROW_PLACES:
         late = lax.shift_right_logical(apart, held[p]) & 1
         entries.append((1, p, jnp.where(late == 1, angles[1, held[p]], 0.0)))
         entries.append((2, p, angles[2, held[p]]))
@@ -296,26 +299,21 @@
     table[0:8, :], table[8:16, :] = turns
     masks = bit_masks()
     for slot, layer, spots, transposed in (
-        (DEVICE_1, 0, DEVICE_ROWS, False),
-        (DEVICE_2, 1, DEVICE_ROWS, False),
-        (DEVICE_3, 2, DEVICE_ROWS, False),
-        (COLUMN_2, 1, LANE_PLACES + [DEVICE_HALF], True),
+        (CHIP_1, 0, CHIP_PLACES, False),
+        (CHIP_2, 1, CHIP_PLACES, False),
+        (CHIP_3, 2, CHIP_PLACES, False),
+        (COLUMN_2, 1, LANE_PLACES + [HALF], True),
         (ROW_2, 1, ROW_PLACES, False),
         (ROW_3, 2, ROW_PLACES, False),
         (COLUMN_3, 2, LANE_PLACES + [HALF], True),
     ):
         high[slot], low[slot] = kron_matrix(masks, turns, layer, spots, transposed)
-    device = lax.axis_index("wide") * lax.axis_size("narrow") + lax.axis_index("narrow")
-
-    def pairs_of(layer, inner):
-        pairs = []
-        for k in range(2 * PAIRS):
-            place = places[pairings[layer, k]]
-            if inner:
-                moved = jnp.where(place >= LOCAL, place - 9, place + 9)
-                place = jnp.where(place < 7, place, moved)
-            pairs.append(place)
-        return list(zip(pairs[::2], pairs[1::2]))
+
+    def pairs_of(layer):
+        return [
+            (places[pairings[layer, 2 * k]], places[pairings[layer, 2 * k + 1]])
+            for k in range(PAIRS)
+        ]
 
     def is_stuck(place):
         mask = jnp.full(place.shape, stuck, jnp.int32)
@@ -325,42 +323,55 @@
         return all_local(p, r) | is_stuck(p) | is_stuck(r)
 
     def on_device(p, r):
-        return ((p >= 7) & (p < LOCAL)) | ((r >= 7) & (r < LOCAL))
+        return (p >= LOCAL) | (r >= LOCAL)
 
     def on_device_not_stuck(p, r):
-        return on_device(p, r) & ~(is_stuck(p - 9) | is_stuck(r - 9))
-
-    sign[SIGN_1] = sign_array(pairs_of(0, True), on_device, device)
-    sign[SIGN_2] = sign_array(pairs_of(1, True), on_device_not_stuck, device)
-    sign[SIGN_LATE] = sign_array(pairs_of(1, False), local_or_stuck, device)
-    sign[SIGN_3] = sign_array(pairs_of(2, False), lambda p, r: p == p, device)
-
-
-def second_kernel(state, high, low, sign, table, out):
+        return on_device(p, r) & ~(is_stuck(p) | is_stuck(r))
+
+    chip = lax.shift_left(lax.shift_right_logical(device, 1) ^ FLIP, 1)
+    mine, other = chip | core, chip | (1 - core)
+    sign[MINE_1] = sign_array(pairs_of(0), on_device, mine, True)
+    sign[OTHER_1] = sign_array(pairs_of(0), on_device, other, True)
+    sign[MINE_2] = sign_array(pairs_of(1), on_device_not_stuck, mine, True)
+    sign[OTHER_2] = sign_array(pairs_of(1), on_device_not_stuck, other, True)
+    sign[SIGN_LATE] = sign_array(pairs_of(1), local_or_stuck, device)
+    sign[SIGN_3] = sign_array(pairs_of(2), lambda p, r: p == p, device)
+
+
+def second_kernel(mine_ref, other_ref, high, low, sign, table, out):
     def matrix(slot):
         return high[slot], low[slot]
 
-    turns = table[0:8, :], table[8:16, :]
-    value = on_rows(matrix(DEVICE_1), load_matrix(state))
-    value = turn_halves(turns, 0, DEVICE_HALF, value) * sign[SIGN_1]
-    value = on_columns(on_rows(matrix(DEVICE_2), value), matrix(COLUMN_2)) * sign[SIGN_2]
-    value = on_rows(matrix(DEVICE_3), value)
-    store_matrix(out, turn_halves(turns, 2, DEVICE_HALF, value))
+    def core_turn(layer):
+        c = table[layer : layer + 1, SIGNED_CORE : SIGNED_CORE + 1]
+        s = table[8 + layer : 9 + layer, SIGNED_CORE : SIGNED_CORE + 1]
+        return c, s
+
+    mine = on_rows(matrix(CHIP_1), load_pieces(mine_ref))
+    other = on_rows(matrix(CHIP_1), load_pieces(other_ref))
+    c, s = core_turn(0)
+    mine, other = c * mine + s * other, c * other - s * mine
+    mine, other = mine * sign[MINE_1], other * sign[OTHER_1]
+    c, s = core_turn(1)
+    mine, other = c * mine + s * other, c * other - s * mine
+    mine = on_columns(on_rows(matrix(CHIP_2), mine), matrix(COLUMN_2)) * sign[MINE_2]
+    other = on_columns(on_rows(matrix(CHIP_2), other), matrix(COLUMN_2)) * sign[OTHER_2]
+    c, s = core_turn(2)
+    store_pieces(out, on_rows(matrix(CHIP_3), c * mine + s * other))
 
 
 def third_kernel(front, back, plan, high, low, sign, table, state, out, work):
     def matrix(slot):
         return high[slot], low[slot]
 
-    turns = table[0:8, :], table[8:16, :]
-    value = load_matrix(state)
     if front:
-        value = on_rows(matrix(ROW_2), value)
-        value = turn_halves(turns, 1, HALF, value) * sign[SIGN_LATE]
+        value = on_rows(matrix(ROW_2), load_pieces(state)) * sign[SIGN_LATE]
         value = on_columns(on_rows(matrix(ROW_3), value), matrix(COLUMN_3))
+    else:
+        value = load_matrix(state)
     if back:
         work[...] = value * sign[SIGN_3]
-        trade_bits(work, [plan[18 + bit] for bit in range(9)])
+        trade_bits(work, [plan[18 + bit] for bit in range(8)])
         value = work[...]
     store_matrix(out, value)
 
@@ -387,8 +398,16 @@
     work = [pltpu.VMEM((SIDE, SIDE), jnp.float32)]
     product_flops = 3 * 2 * SIDE**3
 
+    devices = lax.axis_size(AXES)
+    chips = [[2 * (i ^ FLIP) + core for i in range(devices // 2)] for core in range(2)]
+
     def across(value):
-        return lax.all_to_all(value, AXES, 0, 0, tiled=True)
+        value = value.reshape(SIDE, SIDE)
+        value = lax.all_to_all(value, AXES, 0, 0, tiled=True, axis_index_groups=chips)
+        return value.reshape(rows, LANES)
+
+    def beside(value):
+        return lax.ppermute(value, AXES, [(d, d ^ 1) for d in range(devices)])
 
     fetched = [
         pltpu.VMEM((rows, LANES), jnp.float32),
@@ -399,7 +418,7 @@
     state, plan = call(
         first_kernel,
         [pltpu.HBM] * 3,
-        [flat, ((27,), jnp.int32, S)],
+        [flat, ((26,), jnp.int32, S)],
         work + fetched,
         3 * product_flops,
         60,
@@ -411,7 +430,7 @@
         [
             ((7, SIDE, SIDE), jnp.bfloat16, V),
             ((7, SIDE, SIDE), jnp.bfloat16, V),
-            ((4, SIDE, SIDE), jnp.float32, V),
+            ((6, SIDE, SIDE), jnp.float32, V),
             ((16, LANES), jnp.float32, V),
         ],
         [pltpu.SMEM((25,), jnp.int32)],
@@ -420,8 +439,10 @@
     )(angles, pairings, plan)
     stuck = plan[0] != 0
     state, stuck, prepared = lax.optimization_barrier((state, stuck, prepared))
-    (state,) = call(second_kernel, [V] * 5, [flat], [], 4 * product_flops, 32)(state, *prepared)
-    state = across(state)
+    (state,) = call(second_kernel, [V] * 6, [flat], [], 7 * product_flops, 32)(
+        state, beside(state), *prepared
+    )
+    state, stuck = lax.optimization_barrier((across(state), stuck))
 
     def third(value, front, back):
         kernel = functools.partial(third_kernel, front, back)
@@ -436,7 +457,6 @@
         value = third(value, True, False)
         table = prepared[3]
         device = lax.axis_index(AXES)
-        devices = lax.axis_size(AXES)
         for bit in range(9):
             route = [(d, d ^ 1 << bit) for d in range(devices)]
             other = lax.ppermute(value, AXES, route)

time: 89.6 us -> 85.7 us (0.956)
  waiting for transfers between devices: 44.9 us -> 7.8 us
  blocking collectives: 0 us -> 32.8 us
  Pallas kernels: 9.89 us -> 11.9 us
  starting transfers between devices: 33.9 us -> 32.7 us
    all_to_all x2 -> x1, waiting for transfers between devices: 44.9 us -> 6.66 us  [across(): lax.all_to_all(value, AXES, 0, 0, tiled=True, axis_index_groups=chips)]
    all_to_all x0 -> x1, blocking collectives: none -> 32.8 us  [across(): lax.all_to_all(value, AXES, 0, 0, tiled=True, axis_index_groups=chips)]
    all_to_all x2 -> x1, starting transfers between devices: 33.9 us -> 29.4 us  [across(): lax.all_to_all(value, AXES, 0, 0, tiled=True, axis_index_groups=chips)]
    ppermute x0 -> x1, starting transfers between devices: none -> 3.28 us  [beside(): return lax.ppermute(value, AXES, [(d, d ^ 1) for d in range(devices)])]
    ppermute x0 -> x1, waiting for transfers between devices: none -> 1.14 us  [beside(): return lax.ppermute(value, AXES, [(d, d ^ 1) for d in range(devices)])]
    pallas_call x1, Pallas kernels: 2.12 us -> 3.22 us  [shards(): call(prepare_kernel, [S, S, S], [((7, SIDE, SIDE), jnp.bfloat16, V), ((7,...]
  transfers between devices with their start and end apart: 2 -> 2, of which waited for: 2 -> 2; matrix products, arithmetic and copies ran while one was open for 0% -> 0% of each run, Pallas kernels for 2% -> 4%
where the time goes in v1:
time: 85.7 us; the launch traced here: 85.3 us
  blocking collectives  32.8 us (38%)
  starting transfers between devices  32.7 us (38%)
  Pallas kernels  11.9 us (14%)
  waiting for transfers between devices  7.8 us (9%)
    all_to_all x1, blocking collectives, across(): lax.all_to_all(value, AXES, 0, 0, tiled=True, axis_index_groups=chips)  32.8 us
    all_to_all x1, starting transfers between devices, across(): lax.all_to_all(value, AXES, 0, 0, tiled=True, axis_index_groups=chips)  29.4 us
    all_to_all x1, waiting for transfers between devices, across(): lax.all_to_all(value, AXES, 0, 0, tiled=True, axis_index_groups=chips)  6.66 us
    ppermute x1, starting transfers between devices, beside(): return lax.ppermute(value, AXES, [(d, d ^ 1) for d in range(devices)])  3.28 us
    pallas_call x1, Pallas kernels, shards(): call(prepare_kernel, [S, S, S], [((7, SIDE, SIDE), jnp.bfloat16, V), ((7,...  3.22 us
    pallas_call x1, Pallas kernels, shards(): call(first_kernel, [pltpu.HBM] * 3, [flat, ((26,), jnp.int32, S)], work +...  3.06 us
    pallas_call x1, Pallas kernels, third(): call(kernel, [S] + [V] * 5, [flat], work, 3 * product_flops, 32)  2.82 us
    pallas_call x1, Pallas kernels, shards(): call(second_kernel, [V] * 6, [flat], [], 7 * product_flops, 32)  2.81 us
  transfers between devices with their start and end apart: 2, of which 2 were waited for; matrix products, arithmetic and copies ran while one was open for 0% of the time, Pallas kernels for 4%

profile of v1, /device:TPU:1, one launch (start us, length us, event | category | flops | bytes accessed | tf_op | source)
XLA Modules:
  0.0 85.3 jit_solution(17689112637352469728)
XLA Ops:
  0.0 0.0 copy-start
  0.0 0.0 copy-start.1
  0.0 3.1 %shard_map.39 = (f32[512,128]{1,0:T(8,128)}, s32[26]{0:T(128)S(1)}) custom-call(f32[3,25]{1,0:T(4,128)} %angles.1, s32[3,25]{1,0:T(4,128)} %pairings.1, f32[512,128]{1,0:T(8,128)} %bitcast.34), custom_call_target="tpu_custom_call" | custom-call | flops 301989888 | bytes 4000000 | tf_op jit(solution)/shard_map/pallas_call | solution.py:418
  3.1 29.4 %all-to-all-start = ((f32[256,1,256]{2,1,0:T(1,128)}), f32[256,1,256]{2,1,0:T(1,128)S(1)}, u32[]{:S(2)}, u32[]{:S(2)}) async-start(f32[256,1,256]{2,1,0:T(1,128)} %bitcast.32), calls=%async_computation | async-start | bytes 524288 | tf_op jit(solution)/shard_map/all_to_all | solution.py:406
  32.6 0.0 copy-done
  32.6 0.0 copy-done.1
  32.6 3.2 %shard_map.40 = (bf16[7,256,256]{2,1,0:T(8,128)(2,1)S(1)}, bf16[7,256,256]{2,1,0:T(8,128)(2,1)}, f32[6,256,256]{2,1,0:T(8,128)S(1)}, f32[16,128]{1,0:T(8,128)S(1)}) custom-call(f32[3,25]{1,0:T(4,128)S(1)} %copy-done, s32[3,25]{1,0:T(4,128)S(1)} %copy-done.1, s32[26]{0:T(128)S(1)} %get-tuple-element.59.plan), custom_call_target="tpu_custom_call" | custom-call | flops 4026531840 | bytes 4000000 | tf_op jit(solution)/shard_map/pallas_call | solution.py:427
  35.8 6.7 %all-to-all-done = f32[256,1,256]{2,1,0:T(1,128)S(1)} async-done(((f32[256,1,256]{2,1,0:T(1,128)}), f32[256,1,256]{2,1,0:T(1,128)S(1)}, u32[]{:S(2)}, u32[]{:S(2)}) %all-to-all-start) | async-done | bytes 262176 | tf_op jit(solution)/shard_map/all_to_all | solution.py:406
  42.5 3.3 %collective-permute-start.9 = (f32[512,128]{1,0:T(8,128)S(1)}, f32[512,128]{1,0:T(8,128)S(1)}, u32[]{:S(2)}, u32[]{:S(2)}) collective-permute-start(f32[512,128]{1,0:T(8,128)S(1)} %bitcast.27), channel_id=1, source_target_pairs={{0,1},{1,0},{2,3},{3,2},{4,5},{5,4},{6,7},{7,6},{8,9},{9,8},{10,11... | collective-permute-start | bytes 786440 | tf_op jit(solution)/shard_map/ppermute | solution.py:410
  45.7 1.1 %collective-permute-done.9.other_ref = f32[512,128]{1,0:T(8,128)S(1)} collective-permute-done((f32[512,128]{1,0:T(8,128)S(1)}, f32[512,128]{1,0:T(8,128)S(1)}, u32[]{:S(2)}, u32[]{:S(2)}) %collective-permute-start.9) | collective-permute-done | bytes 262176 | tf_op jit(solution)/shard_map/ppermute | solution.py:410
  46.9 2.8 %shard_map.41 = f32[512,128]{1,0:T(8,128)S(1)} custom-call(f32[512,128]{1,0:T(8,128)S(1)} %bitcast.28, f32[512,128]{1,0:T(8,128)S(1)} %collective-permute-done.9.other_ref, bf16[7,256,256]{2,1,0:T(8,128)(2,1)S(1)} %get-tuple-element.65.high, bf16[7,256,256]{2,1,0:T(8,128)(2,1)} %get-tuple-element.66.low, f32[6,256,256]{2,1,0:T(8,128)S(1)} %get-tuple-element.67.sign, ...), custom_call_target="tpu_custom_call" | custom-call | flops 704643072 | bytes 4000000 | tf_op jit(solution)/shard_map/pallas_call | solution.py:442
  49.7 32.8 %all_to_all.18 = f32[256,1,256]{2,1,0:T(1,128)S(1)} all-to-all(f32[256,1,256]{2,1,0:T(1,128)S(1)} %bitcast.29), channel_id=1, replica_groups={{336,338,340,342,344,346,348,350,320,322,324,326,328,330,332,334,368,37..., dimensions={0} | all-to-all | bytes 524288 | tf_op jit(solution)/shard_map/all_to_all | solution.py:406
  82.5 2.8 %conditional.1 = (f32[65536]{0:T(1024)}) conditional(s32[]{:T(128)} %convert_element_type.3, (s32[26]{0:T(128)S(1)}, bf16[7,256,256]{2,1,0:T(8,128)(2,1)S(1)}, bf16[7,256,256]{2,1,0:T(8,128)(2,1)}, f32[6,256,256]{2,1,0:T(8,128)S(1)}, f32[16,128]{1,0:T(8,128)S(1)}, /*index=5*/f32[512,128]{1,0:T(8,128)S(1)}) %tuple.38, (f32[16,128]{1,0:T(8,128)S(1)}, ...), branch_computations={%region_0.0_spmd, %region_1.2_spmd} | conditional | flops 605749248 | bytes 30283464 | solution.py:468
  82.5 2.8 %branch_0_fun.1 = f32[512,128]{1,0:T(8,128)} custom-call(s32[26]{0:T(128)S(1)} %get-tuple-element.32.plan, bf16[7,256,256]{2,1,0:T(8,128)(2,1)S(1)} %get-tuple-element.33.high, bf16[7,256,256]{2,1,0:T(8,128)(2,1)} %get-tuple-element.34.low, f32[6,256,256]{2,1,0:T(8,128)S(1)} %get-tuple-element.35.sign, f32[16,128]{1,0:T(8,128)S(1)} %get-tuple-element.36.table, ...), custom_call_target="tpu_custom_call" | custom-call | flops 301989888 | bytes 4000000 | tf_op jit(solution)/shard_map/cond/branch_0_fun/pallas_call | solution.py:449
Async XLA Ops:
  0.0 32.6 %copy-start = (f32[3,25]{1,0:T(4,128)S(1)}, f32[3,25]{1,0:T(4,128)}, u32[]{:S(2)}) copy-start(f32[3,25]{1,0:T(4,128)} %angles.1) | copy-start | bytes 904
  0.0 32.6 %copy-start.1 = (s32[3,25]{1,0:T(4,128)S(1)}, s32[3,25]{1,0:T(4,128)}, u32[]{:S(2)}) copy-start(s32[3,25]{1,0:T(4,128)} %pairings.1) | copy-start | bytes 904
  3.1 39.4 %all-to-all-start = ((f32[256,1,256]{2,1,0:T(1,128)}), f32[256,1,256]{2,1,0:T(1,128)S(1)}, u32[]{:S(2)}, u32[]{:S(2)}) async-start(f32[256,1,256]{2,1,0:T(1,128)} %bitcast.32), calls=%async_computation | async-start | bytes 524288 | tf_op jit(solution)/shard_map/all_to_all | solution.py:406
  42.5 4.4 %collective-permute-start.9 = (f32[512,128]{1,0:T(8,128)S(1)}, f32[512,128]{1,0:T(8,128)S(1)}, u32[]{:S(2)}, u32[]{:S(2)}) collective-permute-start(f32[512,128]{1,0:T(8,128)S(1)} %bitcast.27), channel_id=1, source_target_pairs={{0,1},{1,0},{2,3},{3,2},{4,5},{5,4},{6,7},{7,6},{8,9},{9,8},{10,11... | collective-permute-start | bytes 786440 | tf_op jit(solution)/shard_map/ppermute | solution.py:410

commit v2 on v1

--- a/solution.py
+++ b/solution.py
@@ -14,11 +14,13 @@
 SIGNED_CORE = 25
 PAIRS = 12
 FLIP = 0b10101000
+CHIP_BITS = [7, 5, 3, 6, 4, 2, 1, 0]
+ROW_FLIP = sum((FLIP >> bit & 1) << k for k, bit in enumerate(CHIP_BITS))
 AXES = ("wide", "narrow")
 LANE_PLACES = list(range(7))
 ROW_PLACES = list(range(7, 15))
 HALF = 15
-CHIP_PLACES = list(range(17, 25))
+CHIP_PLACES = [17 + bit for bit in CHIP_BITS]
 
 
 def trig(angle):
@@ -155,9 +157,7 @@
             r = jnp.where(spot == k, second, r)
         applies = jnp.where((p >= 0) & keep(p, r), 1, 0)
         if swapped:
-            p, r = (
-                jnp.where(in_rows(x), x + 10, jnp.where(x > CORE, x - 10, x)) for x in (p, r)
-            )
+            p, r = exchanged(p), exchanged(r)
         if device is not None:
             held = jnp.full(shape, device, jnp.int32)
             for place in (p, r):
@@ -172,7 +172,7 @@
         return jnp.where((place >= 0) & (place < 7), place, jnp.where(place == HALF, 7, 8))
 
     p, r, applies = shifts((1, 16), 1)
-    row = iota((SIDE, 16), 0) ^ (FLIP if swapped else 0) | SIDE
+    row = iota((SIDE, 16), 0) ^ (ROW_FLIP if swapped else 0) | SIDE
     row = lax.shift_right_logical(row, jnp.broadcast_to(row_bit(p, applies), row.shape)) & (
         lax.shift_right_logical(row, jnp.broadcast_to(row_bit(r, applies), row.shape))
     )
@@ -191,6 +191,14 @@
 
 def in_rows(place):
     return (place >= 7) & (place < HALF)
+
+
+def exchanged(place):
+    moved = place
+    for row_place, chip_place in zip(ROW_PLACES, CHIP_PLACES):
+        moved = jnp.where(place == row_place, chip_place, moved)
+        moved = jnp.where(place == chip_place, row_place, moved)
+    return moved
 
 
 def all_local(p, r):
@@ -399,7 +407,10 @@
     product_flops = 3 * 2 * SIDE**3
 
     devices = lax.axis_size(AXES)
-    chips = [[2 * (i ^ FLIP) + core for i in range(devices // 2)] for core in range(2)]
+    order = [
+        sum((row >> k & 1) << bit for k, bit in enumerate(CHIP_BITS)) ^ FLIP for row in range(SIDE)
+    ]
+    chips = [[2 * chip + core for chip in order] for core in range(2)]
 
     def across(value):
         value = value.reshape(SIDE, SIDE)

time: 85.7 us -> 83.7 us (0.977)
  blocking collectives: 32.8 us -> 30.9 us
  starting transfers between devices: 32.7 us -> 31.5 us
    all_to_all x1, blocking collectives: 32.8 us -> 30.9 us  [across(): lax.all_to_all(value, AXES, 0, 0, tiled=True, axis_index_groups=chips)]
    all_to_all x1, starting transfers between devices: 29.4 us -> 28.4 us  [across(): lax.all_to_all(value, AXES, 0, 0, tiled=True, axis_index_groups=chips)]
where the time goes in v2:
time: 83.7 us; the launch traced here: 83.3 us
  starting transfers between devices  31.5 us (38%)
  blocking collectives  30.9 us (37%)
  Pallas kernels  12.4 us (15%)
  waiting for transfers between devices  8.5 us (10%)
    all_to_all x1, blocking collectives, across(): lax.all_to_all(value, AXES, 0, 0, tiled=True, axis_index_groups=chips)  30.9 us
    all_to_all x1, starting transfers between devices, across(): lax.all_to_all(value, AXES, 0, 0, tiled=True, axis_index_groups=chips)  28.4 us
    all_to_all x1, waiting for transfers between devices, across(): lax.all_to_all(value, AXES, 0, 0, tiled=True, axis_index_groups=chips)  7.36 us
    pallas_call x1, Pallas kernels, shards(): call(first_kernel, [pltpu.HBM] * 3, [flat, ((26,), jnp.int32, S)], work +...  3.27 us
    pallas_call x1, Pallas kernels, shards(): call(prepare_kernel, [S, S, S], [((7, SIDE, SIDE), jnp.bfloat16, V), ((7,...  3.26 us
    ppermute x1, starting transfers between devices, beside(): return lax.ppermute(value, AXES, [(d, d ^ 1) for d in range(devices)])  3.08 us
    pallas_call x1, Pallas kernels, third(): call(kernel, [S] + [V] * 5, [flat], work, 3 * product_flops, 32)  3.04 us
    pallas_call x1, Pallas kernels, shards(): call(second_kernel, [V] * 6, [flat], [], 7 * product_flops, 32)  2.81 us
  transfers between devices with their start and end apart: 2, of which 2 were waited for; matrix products, arithmetic and copies ran while one was open for 0% of the time, Pallas kernels for 4%

profile of v2, /device:TPU:1, one launch (start us, length us, event | category | flops | bytes accessed | tf_op | source)
XLA Modules:
  0.0 83.3 jit_solution(16369529010481488731)
XLA Ops:
  0.0 0.0 copy-start
  0.0 0.0 copy-start.1
  0.0 3.3 %shard_map.39 = (f32[512,128]{1,0:T(8,128)}, s32[26]{0:T(128)S(1)}) custom-call(f32[3,25]{1,0:T(4,128)} %angles.1, s32[3,25]{1,0:T(4,128)} %pairings.1, f32[512,128]{1,0:T(8,128)} %bitcast.34), custom_call_target="tpu_custom_call" | custom-call | flops 301989888 | bytes 4000000 | tf_op jit(solution)/shard_map/pallas_call | solution.py:429
  3.3 28.4 %all-to-all-start = ((f32[256,1,256]{2,1,0:T(1,128)}), f32[256,1,256]{2,1,0:T(1,128)S(1)}, u32[]{:S(2)}, u32[]{:S(2)}) async-start(f32[256,1,256]{2,1,0:T(1,128)} %bitcast.32), calls=%async_computation | async-start | bytes 524288 | tf_op jit(solution)/shard_map/all_to_all | solution.py:417
  31.7 0.0 copy-done
  31.8 0.0 copy-done.1
  31.8 3.3 %shard_map.40 = (bf16[7,256,256]{2,1,0:T(8,128)(2,1)S(1)}, bf16[7,256,256]{2,1,0:T(8,128)(2,1)}, f32[6,256,256]{2,1,0:T(8,128)S(1)}, f32[16,128]{1,0:T(8,128)S(1)}) custom-call(f32[3,25]{1,0:T(4,128)S(1)} %copy-done, s32[3,25]{1,0:T(4,128)S(1)} %copy-done.1, s32[26]{0:T(128)S(1)} %get-tuple-element.59.plan), custom_call_target="tpu_custom_call" | custom-call | flops 4026531840 | bytes 4000000 | tf_op jit(solution)/shard_map/pallas_call | solution.py:438
  35.0 7.4 %all-to-all-done = f32[256,1,256]{2,1,0:T(1,128)S(1)} async-done(((f32[256,1,256]{2,1,0:T(1,128)}), f32[256,1,256]{2,1,0:T(1,128)S(1)}, u32[]{:S(2)}, u32[]{:S(2)}) %all-to-all-start) | async-done | bytes 262176 | tf_op jit(solution)/shard_map/all_to_all | solution.py:417
  42.4 3.1 %collective-permute-start.9 = (f32[512,128]{1,0:T(8,128)S(1)}, f32[512,128]{1,0:T(8,128)S(1)}, u32[]{:S(2)}, u32[]{:S(2)}) collective-permute-start(f32[512,128]{1,0:T(8,128)S(1)} %bitcast.27), channel_id=1, source_target_pairs={{0,1},{1,0},{2,3},{3,2},{4,5},{5,4},{6,7},{7,6},{8,9},{9,8},{10,11... | collective-permute-start | bytes 786440 | tf_op jit(solution)/shard_map/ppermute | solution.py:421
  45.5 1.1 %collective-permute-done.9.other_ref = f32[512,128]{1,0:T(8,128)S(1)} collective-permute-done((f32[512,128]{1,0:T(8,128)S(1)}, f32[512,128]{1,0:T(8,128)S(1)}, u32[]{:S(2)}, u32[]{:S(2)}) %collective-permute-start.9) | collective-permute-done | bytes 262176 | tf_op jit(solution)/shard_map/ppermute | solution.py:421
  46.6 2.8 %shard_map.41 = f32[512,128]{1,0:T(8,128)S(1)} custom-call(f32[512,128]{1,0:T(8,128)S(1)} %bitcast.28, f32[512,128]{1,0:T(8,128)S(1)} %collective-permute-done.9.other_ref, bf16[7,256,256]{2,1,0:T(8,128)(2,1)S(1)} %get-tuple-element.65.high, bf16[7,256,256]{2,1,0:T(8,128)(2,1)} %get-tuple-element.66.low, f32[6,256,256]{2,1,0:T(8,128)S(1)} %get-tuple-element.67.sign, ...), custom_call_target="tpu_custom_call" | custom-call | flops 704643072 | bytes 4000000 | tf_op jit(solution)/shard_map/pallas_call | solution.py:453
  49.4 30.9 %all_to_all.18 = f32[256,1,256]{2,1,0:T(1,128)S(1)} all-to-all(f32[256,1,256]{2,1,0:T(1,128)S(1)} %bitcast.29), channel_id=1, replica_groups={{336,80,272,16,320,64,256,0,464,208,400,144,448,192,384,128,368,112,304..., dimensions={0} | all-to-all | bytes 524288 | tf_op jit(solution)/shard_map/all_to_all | solution.py:417
  80.3 3.0 %conditional.1 = (f32[65536]{0:T(1024)}) conditional(s32[]{:T(128)} %convert_element_type.3, (s32[26]{0:T(128)S(1)}, bf16[7,256,256]{2,1,0:T(8,128)(2,1)S(1)}, bf16[7,256,256]{2,1,0:T(8,128)(2,1)}, f32[6,256,256]{2,1,0:T(8,128)S(1)}, f32[16,128]{1,0:T(8,128)S(1)}, /*index=5*/f32[512,128]{1,0:T(8,128)S(1)}) %tuple.38, (f32[16,128]{1,0:T(8,128)S(1)}, ...), branch_computations={%region_0.0_spmd, %region_1.2_spmd} | conditional | flops 605749248 | bytes 30283464 | solution.py:479
  80.3 3.0 %branch_0_fun.1 = f32[512,128]{1,0:T(8,128)} custom-call(s32[26]{0:T(128)S(1)} %get-tuple-element.32.plan, bf16[7,256,256]{2,1,0:T(8,128)(2,1)S(1)} %get-tuple-element.33.high, bf16[7,256,256]{2,1,0:T(8,128)(2,1)} %get-tuple-element.34.low, f32[6,256,256]{2,1,0:T(8,128)S(1)} %get-tuple-element.35.sign, f32[16,128]{1,0:T(8,128)S(1)} %get-tuple-element.36.table, ...), custom_call_target="tpu_custom_call" | custom-call | flops 301989888 | bytes 4000000 | tf_op jit(solution)/shard_map/cond/branch_0_fun/pallas_call | solution.py:460
Async XLA Ops:
  0.0 31.7 %copy-start = (f32[3,25]{1,0:T(4,128)S(1)}, f32[3,25]{1,0:T(4,128)}, u32[]{:S(2)}) copy-start(f32[3,25]{1,0:T(4,128)} %angles.1) | copy-start | bytes 904
  0.0 31.8 %copy-start.1 = (s32[3,25]{1,0:T(4,128)S(1)}, s32[3,25]{1,0:T(4,128)}, u32[]{:S(2)}) copy-start(s32[3,25]{1,0:T(4,128)} %pairings.1) | copy-start | bytes 904
  3.3 39.1 %all-to-all-start = ((f32[256,1,256]{2,1,0:T(1,128)}), f32[256,1,256]{2,1,0:T(1,128)S(1)}, u32[]{:S(2)}, u32[]{:S(2)}) async-start(f32[256,1,256]{2,1,0:T(1,128)} %bitcast.32), calls=%async_computation | async-start | bytes 524288 | tf_op jit(solution)/shard_map/all_to_all | solution.py:417
  42.4 4.2 %collective-permute-start.9 = (f32[512,128]{1,0:T(8,128)S(1)}, f32[512,128]{1,0:T(8,128)S(1)}, u32[]{:S(2)}, u32[]{:S(2)}) collective-permute-start(f32[512,128]{1,0:T(8,128)S(1)} %bitcast.27), channel_id=1, source_target_pairs={{0,1},{1,0},{2,3},{3,2},{4,5},{5,4},{6,7},{7,6},{8,9},{9,8},{10,11... | collective-permute-start | bytes 786440 | tf_op jit(solution)/shard_map/ppermute | solution.py:421

commit v3 on v2

--- a/solution.py
+++ b/solution.py
@@ -222,6 +222,21 @@
 
         @pl.when((taken != 0) & (taken < LANES))
         def _():
+            if step >= 8:
+                view = work[...].reshape(SIDE // (2 * step), 2, step, SIDE)
+                for half in range(2):
+                    columns = slice(half * LANES, half * LANES + LANES)
+                    lower = view[:, 0, :, columns].reshape(LANES, LANES)
+                    upper = view[:, 1, :, columns].reshape(LANES, LANES)
+                    lane_up = (iota((LANES, LANES), 1) & taken) != 0
+                    pair = [
+                        jnp.where(lane_up, pltpu.roll(upper, taken, 1), lower),
+                        jnp.where(lane_up, upper, pltpu.roll(lower, LANES - taken, 1)),
+                    ]
+                    shape = (SIDE // (2 * step), 1, step, LANES)
+                    pair = jnp.concatenate([x.reshape(shape) for x in pair], axis=1)
+                    work[:, columns] = pair.reshape(SIDE, LANES)
+                return
             lane_up = (lane & taken) != 0
             row_up = (row & step) != 0
             for half in range(2):
@@ -271,11 +286,15 @@
     store_pieces(out, on_rows(early, work[...]))
 
 
-CHIP_1, CHIP_2, CHIP_3, COLUMN_2, ROW_2, ROW_3, COLUMN_3 = range(7)
-MINE_1, OTHER_1, MINE_2, OTHER_2, SIGN_LATE, SIGN_3 = range(6)
-
-
-def prepare_kernel(angles, pairings, plan, high, low, sign, table, places):
+CHIP_1, CHIP_2, CHIP_3, COLUMN_2 = range(4)
+ROW_2, ROW_3, COLUMN_3 = range(3)
+MINE_1, OTHER_1, MINE_2, OTHER_2 = range(4)
+SIGN_LATE, SIGN_3 = range(2)
+
+
+def prepare_kernel(
+    angles, pairings, plan, high, low, sign, last_high, last_low, last_sign, table, places
+):
     stuck, apart = plan[0], plan[1]
     held = [plan[2 + place] for place in range(LOCAL)]
     waiting = partners_of(pairings, 1, stuck)
@@ -306,16 +325,17 @@
     turns = trig(angle_table(entries))
     table[0:8, :], table[8:16, :] = turns
     masks = bit_masks()
-    for slot, layer, spots, transposed in (
-        (CHIP_1, 0, CHIP_PLACES, False),
-        (CHIP_2, 1, CHIP_PLACES, False),
-        (CHIP_3, 2, CHIP_PLACES, False),
-        (COLUMN_2, 1, LANE_PLACES + [HALF], True),
-        (ROW_2, 1, ROW_PLACES, False),
-        (ROW_3, 2, ROW_PLACES, False),
-        (COLUMN_3, 2, LANE_PLACES + [HALF], True),
+    second, third = (high, low), (last_high, last_low)
+    for (to_high, to_low), slot, layer, spots, transposed in (
+        (second, CHIP_1, 0, CHIP_PLACES, False),
+        (second, CHIP_2, 1, CHIP_PLACES, False),
+        (second, CHIP_3, 2, CHIP_PLACES, False),
+        (second, COLUMN_2, 1, LANE_PLACES + [HALF], True),
+        (third, ROW_2, 1, ROW_PLACES, False),
+        (third, ROW_3, 2, ROW_PLACES, False),
+        (third, COLUMN_3, 2, LANE_PLACES + [HALF], True),
     ):
-        high[slot], low[slot] = kron_matrix(masks, turns, layer, spots, transposed)
+        to_high[slot], to_low[slot] = kron_matrix(masks, turns, layer, spots, transposed)
 
     def pairs_of(layer):
         return [
@@ -342,8 +362,12 @@
     sign[OTHER_1] = sign_array(pairs_of(0), on_device, other, True)
     sign[MINE_2] = sign_array(pairs_of(1), on_device_not_stuck, mine, True)
     sign[OTHER_2] = sign_array(pairs_of(1), on_device_not_stuck, other, True)
-    sign[SIGN_LATE] = sign_array(pairs_of(1), local_or_stuck, device)
-    sign[SIGN_3] = sign_array(pairs_of(2), lambda p, r: p == p, device)
+    last_sign[SIGN_LATE] = sign_array(pairs_of(1), local_or_stuck, device)
+    last_sign[SIGN_3] = sign_array(pairs_of(2), lambda p, r: p == p, device)
+
+
+def begin_kernel(state, high, low, out):
+    out[...] = on_rows((high[CHIP_1], low[CHIP_1]), load_pieces(state))
 
 
 def second_kernel(mine_ref, other_ref, high, low, sign, table, out):
@@ -355,20 +379,21 @@
         s = table[8 + layer : 9 + layer, SIGNED_CORE : SIGNED_CORE + 1]
         return c, s
 
-    mine = on_rows(matrix(CHIP_1), load_pieces(mine_ref))
+    mine = mine_ref[...]
     other = on_rows(matrix(CHIP_1), load_pieces(other_ref))
     c, s = core_turn(0)
     mine, other = c * mine + s * other, c * other - s * mine
     mine, other = mine * sign[MINE_1], other * sign[OTHER_1]
     c, s = core_turn(1)
     mine, other = c * mine + s * other, c * other - s * mine
-    mine = on_columns(on_rows(matrix(CHIP_2), mine), matrix(COLUMN_2)) * sign[MINE_2]
-    other = on_columns(on_rows(matrix(CHIP_2), other), matrix(COLUMN_2)) * sign[OTHER_2]
+    both = jnp.concatenate([on_rows(matrix(CHIP_2), mine), on_rows(matrix(CHIP_2), other)], axis=0)
+    both = on_columns(both, matrix(COLUMN_2))
+    mine, other = both[:SIDE] * sign[MINE_2], both[SIDE:] * sign[OTHER_2]
     c, s = core_turn(2)
     store_pieces(out, on_rows(matrix(CHIP_3), c * mine + s * other))
 
 
-def third_kernel(front, back, plan, high, low, sign, table, state, out, work):
+def third_kernel(front, back, plan, high, low, sign, state, out, work):
     def matrix(slot):
         return high[slot], low[slot]
 
@@ -439,26 +464,32 @@
         prepare_kernel,
         [S, S, S],
         [
-            ((7, SIDE, SIDE), jnp.bfloat16, V),
-            ((7, SIDE, SIDE), jnp.bfloat16, V),
-            ((6, SIDE, SIDE), jnp.float32, V),
+            ((4, SIDE, SIDE), jnp.bfloat16, V),
+            ((4, SIDE, SIDE), jnp.bfloat16, V),
+            ((4, SIDE, SIDE), jnp.float32, V),
+            ((3, SIDE, SIDE), jnp.bfloat16, V),
+            ((3, SIDE, SIDE), jnp.bfloat16, V),
+            ((2, SIDE, SIDE), jnp.float32, V),
             ((16, LANES), jnp.float32, V),
         ],
         [pltpu.SMEM((25,), jnp.int32)],
         40 * product_flops,
-        32,
+        16,
     )(angles, pairings, plan)
     stuck = plan[0] != 0
     state, stuck, prepared = lax.optimization_barrier((state, stuck, prepared))
-    (state,) = call(second_kernel, [V] * 6, [flat], [], 7 * product_flops, 32)(
-        state, beside(state), *prepared
+    square = ((SIDE, SIDE), jnp.float32, V)
+    (begun,) = call(begin_kernel, [V] * 3, [square], [], product_flops, 16)(state, *prepared[:2])
+    table = prepared[6]
+    (state,) = call(second_kernel, [V] * 6, [flat], [], 7 * product_flops, 16)(
+        begun, beside(state), *prepared[:3], table
     )
     state, stuck = lax.optimization_barrier((across(state), stuck))
 
     def third(value, front, back):
         kernel = functools.partial(third_kernel, front, back)
-        return call(kernel, [S] + [V] * 5, [flat], work, 3 * product_flops, 32)(
-            plan, *prepared, value
+        return call(kernel, [S] + [V] * 4, [flat], work, 3 * product_flops, 16)(
+            plan, *prepared[3:6], value
         )[0]
 
     def finish(value):
@@ -466,7 +497,6 @@
 
     def finish_slowly(value):
         value = third(value, True, False)
-        table = prepared[3]
         device = lax.axis_index(AXES)
         for bit in range(9):
             route = [(d, d ^ 1 << bit) for d in range(devices)]

time: 83.7 us -> 81.5 us (0.974)
  Pallas kernels: 12.4 us -> 9.36 us
  local copies, waits for them, and re-layouts: 0.01 us -> 1.34 us
    pallas_call x3 -> x4, Pallas kernels: 9.1 us -> 6.34 us  [the longest x1 3.06 us: shards(): call(prepare_kernel, [S, S, S], [((4, SIDE, SIDE), jnp.bfloat16, V), ((4,...]
    unnamed x4 -> x8, local copies, waits for them, and re-layouts: 0.01 us -> 1.34 us
where the time goes in v3:
time: 81.5 us; the launch traced here: 81.1 us
  starting transfers between devices  31.5 us (39%)
  blocking collectives  31 us (38%)
  Pallas kernels  9.36 us (11%)
  waiting for transfers between devices  7.79 us (10%)
  local copies, waits for them, and re-layouts  1.34 us (2%)
    all_to_all x1, blocking collectives, across(): lax.all_to_all(value, AXES, 0, 0, tiled=True, axis_index_groups=chips)  31 us
    all_to_all x1, starting transfers between devices, across(): lax.all_to_all(value, AXES, 0, 0, tiled=True, axis_index_groups=chips)  28.4 us
    all_to_all x1, waiting for transfers between devices, across(): lax.all_to_all(value, AXES, 0, 0, tiled=True, axis_index_groups=chips)  6.92 us
    ppermute x1, starting transfers between devices, beside(): return lax.ppermute(value, AXES, [(d, d ^ 1) for d in range(devices)])  3.08 us
    pallas_call x1, Pallas kernels, shards(): call(prepare_kernel, [S, S, S], [((4, SIDE, SIDE), jnp.bfloat16, V), ((4,...  3.06 us
    pallas_call x1, Pallas kernels, shards(): call(first_kernel, [pltpu.HBM] * 3, [flat, ((26,), jnp.int32, S)], work +...  3.02 us
  transfers between devices with their start and end apart: 2, of which 2 were waited for; matrix products, arithmetic and copies ran while one was open for 0% of the time, Pallas kernels for 4%

profile of v3, /device:TPU:1, one launch (start us, length us, event | category | flops | bytes accessed | tf_op | source)
XLA Modules:
  0.0 81.1 jit_solution(12346097366119604214)
XLA Ops:
  0.0 3.0 %shard_map.39 = (f32[512,128]{1,0:T(8,128)}, s32[26]{0:T(128)S(1)}) custom-call(f32[3,25]{1,0:T(4,128)} %angles.1, s32[3,25]{1,0:T(4,128)} %pairings.1, f32[512,128]{1,0:T(8,128)} %bitcast.36), custom_call_target="tpu_custom_call" | custom-call | flops 301989888 | bytes 4000000 | tf_op jit(solution)/shard_map/pallas_call | solution.py:454
  3.0 0.0 copy-start.1
  3.0 28.4 %all-to-all-start = ((f32[256,1,256]{2,1,0:T(1,128)}), f32[256,1,256]{2,1,0:T(1,128)S(1)}, u32[]{:S(2)}, u32[]{:S(2)}) async-start(f32[256,1,256]{2,1,0:T(1,128)} %bitcast.32), calls=%async_computation | async-start | bytes 524288 | tf_op jit(solution)/shard_map/all_to_all | solution.py:442
  31.5 0.0 copy-start
  31.5 0.0 copy-done.1
  31.5 0.6 copy-done
  32.1 3.1 %shard_map.40 = (bf16[4,256,256]{2,1,0:T(8,128)(2,1)S(1)}, bf16[4,256,256]{2,1,0:T(8,128)(2,1)S(1)}, f32[4,256,256]{2,1,0:T(8,128)S(1)}, bf16[3,256,256]{2,1,0:T...) custom-call(f32[3,25]{1,0:T(4,128)S(1)} %copy-done, ...), custom_call_target="tpu_custom_call" | custom-call | flops 4026531840 | bytes 4000000 | tf_op jit(solution)/shard_map/pallas_call | solution.py:463
  35.2 6.9 %all-to-all-done = f32[256,1,256]{2,1,0:T(1,128)S(1)} async-done(((f32[256,1,256]{2,1,0:T(1,128)}), f32[256,1,256]{2,1,0:T(1,128)S(1)}, u32[]{:S(2)}, u32[]{:S(2)}) %all-to-all-start) | async-done | bytes 262176 | tf_op jit(solution)/shard_map/all_to_all | solution.py:442
  42.1 3.1 %collective-permute-start.9 = (f32[512,128]{1,0:T(8,128)S(1)}, f32[512,128]{1,0:T(8,128)S(1)}, u32[]{:S(2)}, u32[]{:S(2)}) collective-permute-start(f32[512,128]{1,0:T(8,128)S(1)} %bitcast.27), channel_id=1, source_target_pairs={{0,1},{1,0},{2,3},{3,2},{4,5},{5,4},{6,7},{7,6},{8,9},{9,8},{10,11... | collective-permute-start | bytes 786440 | tf_op jit(solution)/shard_map/ppermute | solution.py:446
  45.2 0.3 shard_map.41.mine_ref
  45.5 0.9 %collective-permute-done.9.other_ref = f32[512,128]{1,0:T(8,128)S(1)} collective-permute-done((f32[512,128]{1,0:T(8,128)S(1)}, f32[512,128]{1,0:T(8,128)S(1)}, u32[]{:S(2)}, u32[]{:S(2)}) %collective-permute-start.9) | collective-permute-done | bytes 262176 | tf_op jit(solution)/shard_map/ppermute | solution.py:446
  46.4 1.5 %shard_map.42 = f32[512,128]{1,0:T(8,128)S(1)} custom-call(f32[256,256]{1,0:T(8,128)S(1)} %shard_map.41.mine_ref, f32[512,128]{1,0:T(8,128)S(1)} %collective-permute-done.9.other_ref, bf16[4,256,256]{2,1,0:T(8,128)(2,1)S(1)} %get-tuple-element.71.high, bf16[4,256,256]{2,1,0:T(8,128)(2,1)S(1)} %get-tuple-element.72.low, ...), custom_call_target="tpu_custom_call" | custom-call | flops 704643072 | bytes 4000000 | tf_op jit(solution)/shard_map/pallas_call | solution.py:484
  47.9 0.0 copy-start.2
  47.9 31.0 %all_to_all.18 = f32[256,1,256]{2,1,0:T(1,128)S(1)} all-to-all(f32[256,1,256]{2,1,0:T(1,128)S(1)} %bitcast.29), channel_id=1, replica_groups={{336,80,272,16,320,64,256,0,464,208,400,144,448,192,384,128,368,112,304..., dimensions={0} | all-to-all | bytes 524288 | tf_op jit(solution)/shard_map/all_to_all | solution.py:442
  78.9 0.0 copy-done.2
  78.9 1.5 %conditional.1 = (f32[65536]{0:T(1024)S(1)}) conditional(s32[]{:T(128)} %convert_element_type.3, (s32[26]{0:T(128)S(1)}, bf16[3,256,256]{2,1,0:T(8,128)(2,1)S(1)}, bf16[3,256,256]{2,1,0:T(8,128)(2,1)S(1)}, f32[2,256,256]{2,1,0:T(8,128)S(1)}, f32[512,128]{1,0:T(8,128)S(1)}) %tuple.40, (f32[16,128]{1,0:T(8,128)S(1)}, s32[26]{0:T(128)S(1)}, ...), branch_computations={%region_0.0_spmd, %region_1.2_spmd} | conditional | flops 605749248 | bytes 24516216 | solution.py:509
  78.9 1.5 %branch_0_fun.1 = f32[512,128]{1,0:T(8,128)S(1)} custom-call(s32[26]{0:T(128)S(1)} %get-tuple-element.30.plan, bf16[3,256,256]{2,1,0:T(8,128)(2,1)S(1)} %get-tuple-element.31.high, bf16[3,256,256]{2,1,0:T(8,128)(2,1)S(1)} %get-tuple-element.32.low, f32[2,256,256]{2,1,0:T(8,128)S(1)} %get-tuple-element.33.sign, f32[512,128]{1,0:T(8,128)S(1)} %get-tuple-element.34.state), custom_call_target="tpu_custom_call" | custom-call | flops 301989888 | bytes 4000000 | tf_op jit(solution)/shard_map/cond/branch_0_fun/pallas_call | solution.py:491
  80.4 0.0 copy-start.3
  80.4 0.7 copy-done.3
Async XLA Ops:
  3.0 28.5 %copy-start.1 = (s32[3,25]{1,0:T(4,128)S(1)}, s32[3,25]{1,0:T(4,128)}, u32[]{:S(2)}) copy-start(s32[3,25]{1,0:T(4,128)} %pairings.1) | copy-start | bytes 904
  3.0 39.1 %all-to-all-start = ((f32[256,1,256]{2,1,0:T(1,128)}), f32[256,1,256]{2,1,0:T(1,128)S(1)}, u32[]{:S(2)}, u32[]{:S(2)}) async-start(f32[256,1,256]{2,1,0:T(1,128)} %bitcast.32), calls=%async_computation | async-start | bytes 524288 | tf_op jit(solution)/shard_map/all_to_all | solution.py:442
  31.5 0.7 copy-start
  42.1 4.2 %collective-permute-start.9 = (f32[512,128]{1,0:T(8,128)S(1)}, f32[512,128]{1,0:T(8,128)S(1)}, u32[]{:S(2)}, u32[]{:S(2)}) collective-permute-start(f32[512,128]{1,0:T(8,128)S(1)} %bitcast.27), channel_id=1, source_target_pairs={{0,1},{1,0},{2,3},{3,2},{4,5},{5,4},{6,7},{7,6},{8,9},{9,8},{10,11... | collective-permute-start | bytes 786440 | tf_op jit(solution)/shard_map/ppermute | solution.py:446
  47.9 31.0 %copy-start.2 = (bf16[3,256,256]{2,1,0:T(8,128)(2,1)S(1)}, bf16[3,256,256]{2,1,0:T(8,128)(2,1)}, u32[]{:S(2)}) copy-start(bf16[3,256,256]{2,1,0:T(8,128)(2,1)} %get-tuple-element.78) | copy-start | bytes 1179652
  80.4 0.7 copy-start.3

commit v4 on v3

--- a/solution.py
+++ b/solution.py
@@ -386,7 +386,8 @@
     mine, other = mine * sign[MINE_1], other * sign[OTHER_1]
     c, s = core_turn(1)
     mine, other = c * mine + s * other, c * other - s * mine
-    both = jnp.concatenate([on_rows(matrix(CHIP_2), mine), on_rows(matrix(CHIP_2), other)], axis=0)
+    both = on_rows(matrix(CHIP_2), jnp.concatenate([mine, other], axis=1))
+    both = jnp.concatenate([both[:, :SIDE], both[:, SIDE:]], axis=0)
     both = on_columns(both, matrix(COLUMN_2))
     mine, other = both[:SIDE] * sign[MINE_2], both[SIDE:] * sign[OTHER_2]
     c, s = core_turn(2)

time: 81.5 us -> 81.6 us (level)
  no operation moved by 1% of the time
where the time goes in v4:
time: 81.6 us; the launch traced here: 81.1 us
  starting transfers between devices  31.5 us (39%)
  blocking collectives  31 us (38%)
  Pallas kernels  9.36 us (11%)
  waiting for transfers between devices  7.79 us (10%)
  local copies, waits for them, and re-layouts  1.34 us (2%)
    all_to_all x1, blocking collectives, across(): lax.all_to_all(value, AXES, 0, 0, tiled=True, axis_index_groups=chips)  31 us
    all_to_all x1, starting transfers between devices, across(): lax.all_to_all(value, AXES, 0, 0, tiled=True, axis_index_groups=chips)  28.4 us
    all_to_all x1, waiting for transfers between devices, across(): lax.all_to_all(value, AXES, 0, 0, tiled=True, axis_index_groups=chips)  6.92 us
    ppermute x1, starting transfers between devices, beside(): return lax.ppermute(value, AXES, [(d, d ^ 1) for d in range(devices)])  3.08 us
    pallas_call x1, Pallas kernels, shards(): call(prepare_kernel, [S, S, S], [((4, SIDE, SIDE), jnp.bfloat16, V), ((4,...  3.06 us
    pallas_call x1, Pallas kernels, shards(): call(first_kernel, [pltpu.HBM] * 3, [flat, ((26,), jnp.int32, S)], work +...  3.02 us
  transfers between devices with their start and end apart: 2, of which 2 were waited for; matrix products, arithmetic and copies ran while one was open for 0% of the time, Pallas kernels for 4%

profile of v4, /device:TPU:1, one launch (start us, length us, event | category | flops | bytes accessed | tf_op | source)
XLA Modules:
  0.0 81.1 jit_solution(12346097366119604214)
XLA Ops:
  0.0 3.0 %shard_map.39 = (f32[512,128]{1,0:T(8,128)}, s32[26]{0:T(128)S(1)}) custom-call(f32[3,25]{1,0:T(4,128)} %angles.1, s32[3,25]{1,0:T(4,128)} %pairings.1, f32[512,128]{1,0:T(8,128)} %bitcast.36), custom_call_target="tpu_custom_call" | custom-call | flops 301989888 | bytes 4000000 | tf_op jit(solution)/shard_map/pallas_call | solution.py:455
  3.0 0.0 copy-start.1
  3.0 28.4 %all-to-all-start = ((f32[256,1,256]{2,1,0:T(1,128)}), f32[256,1,256]{2,1,0:T(1,128)S(1)}, u32[]{:S(2)}, u32[]{:S(2)}) async-start(f32[256,1,256]{2,1,0:T(1,128)} %bitcast.32), calls=%async_computation | async-start | bytes 524288 | tf_op jit(solution)/shard_map/all_to_all | solution.py:443
  31.5 0.0 copy-start
  31.5 0.0 copy-done.1
  31.5 0.6 copy-done
  32.1 3.1 %shard_map.40 = (bf16[4,256,256]{2,1,0:T(8,128)(2,1)S(1)}, bf16[4,256,256]{2,1,0:T(8,128)(2,1)S(1)}, f32[4,256,256]{2,1,0:T(8,128)S(1)}, bf16[3,256,256]{2,1,0:T...) custom-call(f32[3,25]{1,0:T(4,128)S(1)} %copy-done, ...), custom_call_target="tpu_custom_call" | custom-call | flops 4026531840 | bytes 4000000 | tf_op jit(solution)/shard_map/pallas_call | solution.py:464
  35.2 6.9 %all-to-all-done = f32[256,1,256]{2,1,0:T(1,128)S(1)} async-done(((f32[256,1,256]{2,1,0:T(1,128)}), f32[256,1,256]{2,1,0:T(1,128)S(1)}, u32[]{:S(2)}, u32[]{:S(2)}) %all-to-all-start) | async-done | bytes 262176 | tf_op jit(solution)/shard_map/all_to_all | solution.py:443
  42.1 3.1 %collective-permute-start.9 = (f32[512,128]{1,0:T(8,128)S(1)}, f32[512,128]{1,0:T(8,128)S(1)}, u32[]{:S(2)}, u32[]{:S(2)}) collective-permute-start(f32[512,128]{1,0:T(8,128)S(1)} %bitcast.27), channel_id=1, source_target_pairs={{0,1},{1,0},{2,3},{3,2},{4,5},{5,4},{6,7},{7,6},{8,9},{9,8},{10,11... | collective-permute-start | bytes 786440 | tf_op jit(solution)/shard_map/ppermute | solution.py:447
  45.2 0.3 shard_map.41.mine_ref
  45.5 0.9 %collective-permute-done.9.other_ref = f32[512,128]{1,0:T(8,128)S(1)} collective-permute-done((f32[512,128]{1,0:T(8,128)S(1)}, f32[512,128]{1,0:T(8,128)S(1)}, u32[]{:S(2)}, u32[]{:S(2)}) %collective-permute-start.9) | collective-permute-done | bytes 262176 | tf_op jit(solution)/shard_map/ppermute | solution.py:447
  46.4 1.5 %shard_map.42 = f32[512,128]{1,0:T(8,128)S(1)} custom-call(f32[256,256]{1,0:T(8,128)S(1)} %shard_map.41.mine_ref, f32[512,128]{1,0:T(8,128)S(1)} %collective-permute-done.9.other_ref, bf16[4,256,256]{2,1,0:T(8,128)(2,1)S(1)} %get-tuple-element.71.high, bf16[4,256,256]{2,1,0:T(8,128)(2,1)S(1)} %get-tuple-element.72.low, ...), custom_call_target="tpu_custom_call" | custom-call | flops 704643072 | bytes 4000000 | tf_op jit(solution)/shard_map/pallas_call | solution.py:485
  47.9 0.0 copy-start.2
  47.9 31.0 %all_to_all.18 = f32[256,1,256]{2,1,0:T(1,128)S(1)} all-to-all(f32[256,1,256]{2,1,0:T(1,128)S(1)} %bitcast.29), channel_id=1, replica_groups={{336,80,272,16,320,64,256,0,464,208,400,144,448,192,384,128,368,112,304..., dimensions={0} | all-to-all | bytes 524288 | tf_op jit(solution)/shard_map/all_to_all | solution.py:443
  78.9 0.0 copy-done.2
  78.9 1.5 %conditional.1 = (f32[65536]{0:T(1024)S(1)}) conditional(s32[]{:T(128)} %convert_element_type.3, (s32[26]{0:T(128)S(1)}, bf16[3,256,256]{2,1,0:T(8,128)(2,1)S(1)}, bf16[3,256,256]{2,1,0:T(8,128)(2,1)S(1)}, f32[2,256,256]{2,1,0:T(8,128)S(1)}, f32[512,128]{1,0:T(8,128)S(1)}) %tuple.40, (f32[16,128]{1,0:T(8,128)S(1)}, s32[26]{0:T(128)S(1)}, ...), branch_computations={%region_0.0_spmd, %region_1.2_spmd} | conditional | flops 605749248 | bytes 24516216 | solution.py:510
  78.9 1.5 %branch_0_fun.1 = f32[512,128]{1,0:T(8,128)S(1)} custom-call(s32[26]{0:T(128)S(1)} %get-tuple-element.30.plan, bf16[3,256,256]{2,1,0:T(8,128)(2,1)S(1)} %get-tuple-element.31.high, bf16[3,256,256]{2,1,0:T(8,128)(2,1)S(1)} %get-tuple-element.32.low, f32[2,256,256]{2,1,0:T(8,128)S(1)} %get-tuple-element.33.sign, f32[512,128]{1,0:T(8,128)S(1)} %get-tuple-element.34.state), custom_call_target="tpu_custom_call" | custom-call | flops 301989888 | bytes 4000000 | tf_op jit(solution)/shard_map/cond/branch_0_fun/pallas_call | solution.py:492
  80.4 0.0 copy-start.3
  80.4 0.7 copy-done.3
Async XLA Ops:
  3.0 28.5 %copy-start.1 = (s32[3,25]{1,0:T(4,128)S(1)}, s32[3,25]{1,0:T(4,128)}, u32[]{:S(2)}) copy-start(s32[3,25]{1,0:T(4,128)} %pairings.1) | copy-start | bytes 904
  3.0 39.1 %all-to-all-start = ((f32[256,1,256]{2,1,0:T(1,128)}), f32[256,1,256]{2,1,0:T(1,128)S(1)}, u32[]{:S(2)}, u32[]{:S(2)}) async-start(f32[256,1,256]{2,1,0:T(1,128)} %bitcast.32), calls=%async_computation | async-start | bytes 524288 | tf_op jit(solution)/shard_map/all_to_all | solution.py:443
  31.5 0.7 copy-start
  42.1 4.2 %collective-permute-start.9 = (f32[512,128]{1,0:T(8,128)S(1)}, f32[512,128]{1,0:T(8,128)S(1)}, u32[]{:S(2)}, u32[]{:S(2)}) collective-permute-start(f32[512,128]{1,0:T(8,128)S(1)} %bitcast.27), channel_id=1, source_target_pairs={{0,1},{1,0},{2,3},{3,2},{4,5},{5,4},{6,7},{7,6},{8,9},{9,8},{10,11... | collective-permute-start | bytes 786440 | tf_op jit(solution)/shard_map/ppermute | solution.py:447
  47.9 31.0 %copy-start.2 = (bf16[3,256,256]{2,1,0:T(8,128)(2,1)S(1)}, bf16[3,256,256]{2,1,0:T(8,128)(2,1)}, u32[]{:S(2)}) copy-start(bf16[3,256,256]{2,1,0:T(8,128)(2,1)} %get-tuple-element.78) | copy-start | bytes 1179652
  80.4 0.7 copy-start.3
